TPU v7x, 512 devices: a whole 4x8x8 slice. The times are simulated.
512 devices in a mesh: wide: 64 (over z, y), narrow: 8 (over x, core).
Axes of the slice: x: 4, y: 8, z: 8, core: 2. Of those that a mesh axis runs over, the one named last changes fastest.
Arguments:
- matrix: bfloat16 [16384, 16384], P('wide', 'narrow'), may hold values from 0.002 to 18
- in_rows: int32 [64, 4], replicated, may hold values from 0 to 63, all different within a row; in each aligned block of 8 rows (0 to 7, 8 to 15, ...) no two rows name the same one
- keep: int32 [64, 4, 2], replicated, may hold values 0 or 1
Outputs:
- clustered: bfloat16 [16384, 16384], P('wide', 'narrow')
Inputs may be any that keep to these rules, and one draw needn't show every extreme that they name: `in_rows`: each row names 4 different tile rows. In each aligned block of 8 rows (the tile columns of one index of narrow) no tile row is named by more than 1 row, and some tile row is named by exactly 1.
All inputs are finite; a program needn't handle non-finite values.
Results may differ from a plain program's by a relative error of at most 0.001.
Values may be sent and summed in bfloat16 or wider, within the bound.
A program may use at most 128 MiB of HBM per device.

v0:
```python
import jax
import jax.numpy as jnp
from jax import lax
from jax.sharding import PartitionSpec as P

TILE = 256


def slot_onehot(holds, capacity):
    ranking = jnp.cumsum(holds.astype(jnp.int32), axis=-1) - 1
    levels = jnp.arange(capacity, dtype=jnp.int32)
    return holds[..., None, :] & (ranking[..., None, :] == levels[:, None])


def panel_product(
    column_panel, row_panel, tile_cols, own_rows, onehot_column, wide_ids, col_ids, columns, fan_in
):
    needed = own_rows.reshape(-1)
    chooser_row = (tile_cols[None, :] == needed[:, None]).astype(jnp.bfloat16)
    left_tiles = jnp.einsum(
        "xa,aij->xij", chooser_row, row_panel, preferred_element_type=jnp.float32
    ).astype(jnp.bfloat16)
    column_of = jnp.repeat(col_ids, fan_in)
    slot_owner = jnp.transpose(onehot_column, (2, 0, 1))[column_of]
    chooser_col = (
        ((wide_ids[None, :, None] == needed[:, None, None]) & slot_owner)
        .reshape(needed.shape[0], -1)
        .astype(jnp.bfloat16)
    )
    right_tiles = jnp.einsum(
        "xb,bij->xij", chooser_col, column_panel, preferred_element_type=jnp.float32
    ).astype(jnp.bfloat16)
    products = jnp.einsum(
        "xij,xjl->xil", left_tiles, right_tiles, preferred_element_type=jnp.float32
    )
    return jnp.sum(products.reshape(columns, fan_in, TILE, TILE), axis=1)


def on_device(matrix, in_rows, keep):
    wide_count = lax.axis_size("wide")
    narrow_count = lax.axis_size("narrow")
    row_index = lax.axis_index("wide")
    col_block = lax.axis_index("narrow")
    columns = matrix.shape[1] // TILE
    fan_in = in_rows.shape[1]
    total_cols = in_rows.shape[0]
    keep_width = keep.shape[2]
    capacity = max(1, (columns * fan_in + total_cols - 1) // total_cols)
    blocks = in_rows.reshape(narrow_count, columns, fan_in)
    own_rows = blocks[col_block]
    own_keep = keep.reshape(narrow_count, columns, fan_in, keep_width)[col_block]
    wide_ids = jnp.arange(wide_count, dtype=jnp.int32)
    col_ids = jnp.arange(columns, dtype=jnp.int32)
    holds_column = jnp.any(own_rows[None, :, :] == wide_ids[:, None, None], axis=2)
    onehot_column = slot_onehot(holds_column, capacity)
    holds_row = jnp.any(blocks == row_index, axis=2)
    onehot_row = slot_onehot(holds_row, capacity)
    block_starts = jnp.arange(narrow_count, dtype=jnp.int32)[:, None] * columns
    tile_cols = jnp.where(
        jnp.any(onehot_row, axis=2),
        jnp.sum(jnp.where(onehot_row, col_ids, 0), axis=2) + block_starts,
        -1,
    ).reshape(-1)
    own_slots = onehot_column[row_index]
    local_tiles = matrix.reshape(TILE, columns, TILE)
    packed = jnp.einsum(
        "cq,iqj->cij",
        own_slots.astype(jnp.bfloat16),
        local_tiles,
        preferred_element_type=jnp.float32,
    ).astype(jnp.bfloat16)
    row_panel = lax.all_gather(packed, "narrow", axis=0, tiled=True)
    column_panel = lax.all_gather(packed, "wide", axis=0, tiled=True)
    product = panel_product(
        column_panel,
        row_panel,
        tile_cols,
        own_rows,
        onehot_column,
        wide_ids,
        col_ids,
        columns,
        fan_in,
    )
    candidates = in_rows[own_rows][:, :, :keep_width]
    forced = (jnp.arange(fan_in, dtype=jnp.int32)[:, None] == 0) & (
        jnp.arange(keep_width, dtype=jnp.int32)[None, :] == 0
    )
    chosen = (own_keep == 1) | forced[None, :, :]
    kept_rows = jnp.any((candidates == row_index) & chosen, axis=(1, 2))
    pruned = jnp.where(kept_rows[:, None, None], product, jnp.float32(0.0))
    inflated = pruned * pruned
    local_sum = jnp.sum(inflated, axis=1).reshape(-1)
    totals = lax.psum(local_sum, "wide")
    scaled = TILE * inflated / totals.reshape(columns, 1, TILE)
    return jnp.transpose(scaled, (1, 0, 2)).reshape(TILE, columns * TILE).astype(jnp.bfloat16)


def solution(mesh):
    in_specs = (P("wide", "narrow"), P(), P())
    out_specs = P("wide", "narrow")
    return jax.shard_map(
        on_device, mesh=mesh, in_specs=in_specs, out_specs=out_specs, check_vma=False
    )
```

profile of v0, /device:TPU:6, one launch (start us, length us, event | category | flops | bytes accessed | tf_op | source)
XLA Modules:
  0.0 317.7 jit_solution(12412853887967395596)
XLA Ops:
  6.5 0.8 reshape.204
  7.4 1.5 copy.62
  9.0 0.2 dynamic-slice_reduce_fusion
  9.2 0.4 fusion.27
  9.6 0.7 copy.81
  10.3 0.7 all-gather.7.cloned.1.call-update
  11.0 0.8 copy.46
  11.8 0.7 compare_reduce_fusion
  12.6 0.2 reduce_window_sum.22
  13.4 0.6 gather_fusion
  14.0 0.1 copy.60
  14.3 0.1 reduce_or.43
  14.4 0.6 gather_fusion.1
  15.1 0.1 and_reduce_fusion
  15.2 27.3 %all-gather.5.cloned.1.call-done = bf16[2048,256]{1,0:T(8,128)(2,1)} async-done(((bf16[256,256]{1,0:T(8,128)(2,1)}), bf16[2048,256]{1,0:T(8,128)(2,1)}) %all-gather.5.cloned.1.call-update) | async-done | bytes 1048592 | tf_op jit(solution)/shard_map/all_gather | solution.py:72
  42.5 4.6 %convolution_convert_fusion = bf16[32,256,256]{2,0,1:T(8,128)(2,1)} fusion(bf16[8,256,256]{2,1,0:T(8,128)(2,1)} %bitcast.52, s32[32]{0:T(128)S(1)} %eq.121, s32[8]{0:T(128)S(1)} %add_select_fusion), kind=kOutput, calls=%fused_computation.9 | convolution fusion | flops 35651840 | bytes 5243040 | tf_op jit(solution)/shard_map/xa,aij->xij/dot_general | solution.py:20
  47.0 99.1 %all-gather.7.cloned.1.call-done = bf16[16384,256]{1,0:T(8,128)(2,1)} async-done(((bf16[256,256]{1,0:T(8,128)(2,1)}), bf16[16384,256]{1,0:T(8,128)(2,1)}) %all-gather.7.cloned.1.call-update) | async-done | bytes 8388624 | tf_op jit(solution)/shard_map/all_gather | solution.py:73
  146.1 9.5 %fusion.5 = bf16[32,256,256]{2,0,1:T(8,128)(2,1)S(1)} fusion(bf16[64,256,256]{2,1,0:T(8,128)(2,1)} %bitcast.45, pred[32,64]{1,0:T(32,128)(4,1)S(1)} %gather_fusion.1, s32[32]{0:T(128)S(1)} %eq.121), kind=kOutput, calls=%fused_computation.8 | convolution fusion | flops 270536704 | bytes 12585088 | tf_op jit(solution)/shard_map/xb,bij->xij/dot_general | solution.py:30
  155.6 9.0 %bitcast_reduce_fusion = f32[8,256,256]{2,1,0:T(8,128)S(1)} fusion(bf16[32,256,256]{2,0,1:T(8,128)(2,1)S(1)} %fusion.5, bf16[32,256,256]{2,0,1:T(8,128)(2,1)S(1)} %copy-done), kind=kOutput, calls=%fused_computation.2 | convolution fusion | flops 1075314688 | bytes 10485760 | tf_op jit(solution)/shard_map/xij,xjl->xil/dot_general | solution.py:33
  164.6 0.3 fusion.12
  164.9 143.7 %psum.7 = f32[8,256]{1,0:T(8,128)S(1)} all-reduce(f32[8,256]{1,0:T(8,128)S(1)} %fusion.12), channel_id=1, replica_groups=mesh['wide'=64,'narrow'=8] {'wide'}, use_global_device_ids=true, to_apply=%region_9.10 | all-reduce | flops 2048 | bytes 16384 | tf_op jit(solution)/shard_map/psum | solution.py:94
  308.6 0.4 fusion.14
  308.9 0.5 copy.55
  309.5 1.4 copy.56
  (33 shorter events, 1.1 us)
Async XLA Ops:
  6.5 6.7 %copy-start.1 = (s32[64,4,2]{0,2,1:T(2,128)S(1)}, s32[64,4,2]{0,2,1:T(2,128)}, u32[]{:S(2)}) copy-start(s32[64,4,2]{0,2,1:T(2,128)} %param.5) | copy-start | bytes 6148
  6.5 36.0 %all-gather.5.cloned.1.call-start = ((), (), s32[]{:S(2)}) async-start(), calls=%async_computation | async-start | bytes 1179648 | tf_op jit(solution)/shard_map/all_gather | solution.py:72
  10.3 135.8 %all-gather.7.cloned.1.call-start = ((), (), s32[]{:S(2)}) async-start(), calls=%async_computation.1 | async-start | bytes 8519680 | tf_op jit(solution)/shard_map/all_gather | solution.py:73
  146.1 9.5 %copy-start = (bf16[32,256,256]{2,0,1:T(8,128)(2,1)S(1)}, bf16[32,256,256]{2,0,1:T(8,128)(2,1)}, u32[]{:S(2)}) copy-start(bf16[32,256,256]{2,0,1:T(8,128)(2,1)} %convolution_convert_fusion) | copy-start | bytes 12582916
Sparse Core Ops, SparseCore 0:
  10.4 32.0 all-gather.4
  45.6 100.5 all-gather.6
where the time goes:
time: 318 us
  blocking collectives  144 us (45%)
  waiting for transfers between devices  127 us (40%)
  matrix products  23.4 us (7%)
  between operations  13.5 us (4%)
  local copies, waits for them, and re-layouts  7.89 us (2%)
    psum x1, blocking collectives, on_device(): totals = lax.psum(local_sum, 'wide')  144 us
    all_gather x1, waiting for transfers between devices, on_device(): column_panel = lax.all_gather(packed, 'wide', axis=0, tiled=True)  99.1 us
    all_gather x1, waiting for transfers between devices, on_device(): row_panel = lax.all_gather(packed, 'narrow', axis=0, tiled=True)  27.3 us
    dot_general x1, matrix products, panel_product(): jnp.einsum('xb,bij->xij', chooser_col, column_panel, preferred_element_ty...  9.46 us
    dot_general x1, matrix products, panel_product(): jnp.einsum('xij,xjl->xil', left_tiles, right_tiles, preferred_element_typ...  8.99 us
  transfers between devices with their start and end apart: 2, of which 2 were waited for; matrix products, arithmetic and copies ran while one was open for 3% of the time, Pallas kernels for 0%

commit v1 on v0

v1 whole, which is shorter than its diff:
```python
import jax
import jax.numpy as jnp
from jax import lax
from jax.experimental import pallas as pl
from jax.experimental.pallas import tpu as pltpu
from jax.sharding import PartitionSpec as P

TILE = 256
RING = 8
COLS = 8
FAN = 4
KEEP = 2
CHUNKS = 2
HEIGHT = TILE // CHUNKS
MESH = pl.DeviceIdType.MESH


def kernel(
    in_rows,
    keep,
    matrix,
    out,
    cols,
    outgoing,
    slots,
    panel,
    infl,
    sums,
    result,
    load_sem,
    store_sem,
    y_send,
    y_recv,
    z_send,
    z_recv,
    x_send,
    x_recv,
    t_send,
    t_recv,
    *rings,
):
    row = lax.axis_index("wide")
    block = lax.axis_index("narrow")
    z = row // RING
    y = row % RING

    def along_y(step):
        return {"wide": z * RING + (y + step + RING) % RING}

    def along_z(step):
        return {"wide": ((z + step + RING) % RING) * RING + y}

    def along_x(step):
        return {"narrow": (block + step) % COLS}

    barrier = pltpu.get_barrier_semaphore()
    for step in range(1, RING):
        for target in (along_y(step), along_z(step), along_x(step)):
            pl.semaphore_signal(barrier, inc=1, device_id=target, device_id_type=MESH)
    loads = []
    for col in range(COLS):
        load = pltpu.make_async_copy(
            matrix.at[:, pl.ds(col * TILE, TILE)], cols.at[col], load_sem.at[col]
        )
        load.start()
        loads.append(load)

    mine = jnp.int32(0)
    for col in range(COLS):
        for s in range(FAN):
            mine = jnp.where(in_rows[block * COLS + col, s] == row, col, mine)
    holder = [jnp.int32(0) for _ in range(RING)]
    for k in range(RING):
        for t in range(FAN):
            named = in_rows[z * RING + k, t]
            for d in range(RING):
                hit = named == ((z + d) % RING) * RING + y
                holder[d] = jnp.where(hit, (k - y + RING) % RING, holder[d])

    for load in loads:
        load.wait()
    slots[RING] = jnp.zeros((TILE, TILE), jnp.bfloat16)
    own = cols[mine]
    for chunk, ring in enumerate(rings):
        ring[0] = own[chunk * HEIGHT : (chunk + 1) * HEIGHT]
    panel[0] = own
    pl.semaphore_wait(barrier, 3 * (RING - 1))

    started = []

    def send(src, dst, send_sem, recv_sem, target):
        copy = pltpu.make_async_remote_copy(
            src_ref=src,
            dst_ref=dst,
            send_sem=send_sem,
            recv_sem=recv_sem,
            device_id=target,
            device_id_type=MESH,
        )
        copy.start()
        started.append(copy)
        return copy

    half = HEIGHT // 2
    moves = {}

    def ring_step(chunk, step):
        ring = rings[chunk]
        up = pl.ds(0, HEIGHT if step < 4 else half)
        down = pl.ds(0, HEIGHT) if step < 4 else pl.ds(half, half)
        if step > 1:
            for copy in moves[chunk, step - 1]:
                copy.wait_recv()
        moves[chunk, step] = (
            send(
                ring.at[(1 - step) % RING, up],
                ring.at[-step % RING, up],
                y_send.at[chunk, 0, step - 1],
                y_recv.at[chunk, 0, step - 1],
                along_y(1),
            ),
            send(
                ring.at[step - 1, down],
                ring.at[step, down],
                y_send.at[chunk, 1, step - 1],
                y_recv.at[chunk, 1, step - 1],
                along_y(-1),
            ),
        )

    across = []

    def hand_out(chunk):
        for copy in moves[chunk, 4]:
            copy.wait_recv()
        ring = rings[chunk]
        rows = pl.ds(chunk * HEIGHT, HEIGHT)
        for d in (4, 3, 5, 2, 6, 1, 7):
            outgoing[d, rows] = ring[holder[d]]
            across.append(
                send(
                    outgoing.at[d, rows],
                    slots.at[-d % RING, rows],
                    z_send.at[chunk, d - 1],
                    z_recv.at[chunk, d - 1],
                    along_z(d),
                )
            )
        slots[0, rows] = ring[holder[0]]

    for wave in range(CHUNKS + 5):
        for chunk in range(CHUNKS):
            step = wave - chunk
            if 1 <= step <= 4:
                ring_step(chunk, step)
            if step == 5:
                hand_out(chunk)
        if wave == 1:
            gathers = [
                send(
                    panel.at[0],
                    panel.at[-d % COLS],
                    x_send.at[d - 1],
                    x_recv.at[d - 1],
                    along_x(d),
                )
                for d in (4, 3, 5, 2, 6, 1, 7)
            ]

    lefts, rights, kept = [], [], []
    for col in range(COLS):
        column = block * COLS + col
        is_kept = jnp.bool_(False)
        for s in range(FAN):
            inner = in_rows[column, s]
            meets = jnp.bool_(False)
            for t in range(FAN):
                names = in_rows[inner, t] == row
                meets = meets | names
                if t < KEEP:
                    if s == 0 and t == 0:
                        is_kept = is_kept | names
                    else:
                        is_kept = is_kept | (names & (keep[column, s, t] == 1))
            group = inner // RING
            lefts.append((group - block + COLS) % COLS)
            rights.append(jnp.where(meets, (group - z + RING) % RING, RING))
        kept.append(is_kept)

    for copy in gathers:
        copy.wait_recv()
    for copy in across:
        copy.wait_recv()

    for col in range(COLS):
        total = jnp.zeros((TILE, TILE), jnp.float32)
        for s in range(FAN):
            i = col * FAN + s
            total += jnp.dot(
                panel[lefts[i]], slots[rights[i]], preferred_element_type=jnp.float32
            )
        total = jnp.where(kept[col], total, jnp.float32(0.0))
        square = total * total
        infl[col] = square
        sums[0, pl.ds(col, 1)] = jnp.sum(square, axis=0, keepdims=True)

    def add_up(first, move):
        copies = [
            send(
                sums.at[first],
                sums.at[first + d],
                t_send.at[first + d - 1],
                t_recv.at[first + d - 1],
                move(d),
            )
            for d in range(1, RING)
        ]
        for copy in copies:
            copy.wait_recv()
        total = sums[first]
        for d in range(1, RING):
            total += sums[first + d]
        return total

    sums[RING] = add_up(0, along_y)
    scale = jnp.float32(TILE) / add_up(RING, along_z)

    stores = []
    for col in range(COLS):
        result[col] = (infl[col] * scale[col : col + 1]).astype(jnp.bfloat16)
        store = pltpu.make_async_copy(
            result.at[col], out.at[:, pl.ds(col * TILE, TILE)], store_sem.at[col]
        )
        store.start()
        stores.append(store)
    for copy in started:
        copy.wait_send()
    for store in stores:
        store.wait()


def on_device(matrix, in_rows, keep):
    tile = (TILE, TILE)
    dma = pltpu.SemaphoreType.DMA
    return pl.pallas_call(
        kernel,
        out_shape=jax.ShapeDtypeStruct(matrix.shape, jnp.bfloat16),
        in_specs=[
            pl.BlockSpec(memory_space=pltpu.SMEM),
            pl.BlockSpec(memory_space=pltpu.SMEM),
            pl.BlockSpec(memory_space=pl.ANY),
        ],
        out_specs=pl.BlockSpec(memory_space=pl.ANY),
        scratch_shapes=[
            pltpu.VMEM((COLS, *tile), jnp.bfloat16),
            pltpu.VMEM((RING, *tile), jnp.bfloat16),
            pltpu.VMEM((RING + 1, *tile), jnp.bfloat16),
            pltpu.VMEM((COLS, *tile), jnp.bfloat16),
            pltpu.VMEM((COLS, *tile), jnp.float32),
            pltpu.VMEM((2 * RING, COLS, TILE), jnp.float32),
            pltpu.VMEM((COLS, *tile), jnp.bfloat16),
            dma((COLS,)),
            dma((COLS,)),
            dma((CHUNKS, 2, 4)),
            dma((CHUNKS, 2, 4)),
            dma((CHUNKS, RING - 1)),
            dma((CHUNKS, RING - 1)),
            dma((COLS - 1,)),
            dma((COLS - 1,)),
            dma((2 * RING - 1,)),
            dma((2 * RING - 1,)),
            *[pltpu.VMEM((RING, HEIGHT, TILE), jnp.bfloat16)] * CHUNKS,
        ],
        compiler_params=pltpu.CompilerParams(
            collective_id=0, has_side_effects=True, vmem_limit_bytes=40 << 20
        ),
    )(in_rows, keep, matrix)


def solution(mesh):
    return jax.shard_map(
        on_device,
        mesh=mesh,
        in_specs=(P("wide", "narrow"), P(), P()),
        out_specs=P("wide", "narrow"),
        check_vma=False,
    )
```

time: 318 us -> 70 us (0.22)
  blocking collectives: 144 us -> 0 us
  waiting for transfers between devices: 127 us -> 0 us
  Pallas kernels: 0 us -> 66.7 us
  matrix products: 23.4 us -> 0 us
  between operations: 13.5 us -> 0.03 us
  local copies, waits for them, and re-layouts: 7.89 us -> 3.11 us
    psum x1 -> x0, blocking collectives: 144 us -> none  [on_device(): totals = lax.psum(local_sum, 'wide')]
    all_gather x2 -> x0, waiting for transfers between devices: 126 us -> none  [the longest x1 99.1 us: on_device(): column_panel = lax.all_gather(packed, 'wide', axis=0, tiled=True)]
    pallas_call x0 -> x1, Pallas kernels: none -> 66.7 us  [on_device(): pl.pallas_call(kernel, out_shape=jax.ShapeDtypeStruct(matrix.shape, jnp.b...]
    dot_general x4 -> x0, matrix products: 23.4 us -> none  [the longest x1 9.46 us: panel_product(): jnp.einsum('xb,bij->xij', chooser_col, column_panel, preferred_element_ty...]
  transfers between devices with their start and end apart: 2 -> 0, of which waited for: 2 -> 0; matrix products, arithmetic and copies ran while one was open for 3% -> 0% of each run, Pallas kernels for 0% -> 0%
where the time goes in v1:
time: 70 us; the launch traced here: 69.8 us
  Pallas kernels  66.7 us (95%)
  local copies, waits for them, and re-layouts  3.11 us (4%)
    pallas_call x1, Pallas kernels, on_device(): pl.pallas_call(kernel, out_shape=jax.ShapeDtypeStruct(matrix.shape, jnp.b...  66.7 us
    unnamed x7, local copies, waits for them, and re-layouts  3.11 us

profile of v1, /device:TPU:6, one launch (start us, length us, event | category | flops | bytes accessed | tf_op | source)
XLA Modules:
  0.0 69.8 jit_solution(2232452234729370199)
XLA Ops:
  0.0 0.0 copy-start.1
  0.0 0.8 %copy.4.in_rows = s32[64,4]{1,0:T(8,128)S(1)} copy(s32[64,4]{0,1:T(4,128)} %param.4) | data formatting | bytes 2048 | tf_op args[1]
  0.8 0.0 copy-done.1
  0.8 0.1 copy.5.keep
  0.9 0.0 copy-start
  0.9 1.2 %copy-done = bf16[256,2048]{1,0:T(8,128)(2,1)S(1)} copy-done((bf16[256,2048]{1,0:T(8,128)(2,1)S(1)}, bf16[256,2048]{1,0:T(8,128)(2,1)}, u32[]{:S(2)}) %copy-start) | copy-done | bytes 1048600
  2.2 66.7 %shard_map.37 = bf16[256,2048]{1,0:T(8,128)(2,1)S(1)} custom-call(s32[64,4]{1,0:T(8,128)S(1)} %copy.4.in_rows, s32[64,4,2]{2,1,0:T(4,128)S(1)} %copy.5.keep, bf16[256,2048]{1,0:T(8,128)(2,1)S(1)} %copy-done), custom_call_target="tpu_custom_call" | custom-call | tf_op jit(solution)/shard_map/pallas_call | solution.py:245
  68.9 1.0 %copy.7 = bf16[256,2048]{1,0:T(8,128)(2,1)} copy(bf16[256,2048]{1,0:T(8,128)(2,1)S(1)} %shard_map.37) | data formatting | bytes 2097152
Async XLA Ops:
  0.0 0.8 %copy-start.1 = (s32[64,4,2]{0,2,1:T(2,128)S(1)}, s32[64,4,2]{0,2,1:T(2,128)}, u32[]{:S(2)}) copy-start(s32[64,4,2]{0,2,1:T(2,128)} %param.5) | copy-start | bytes 6148
  0.9 1.2 %copy-start = (bf16[256,2048]{1,0:T(8,128)(2,1)S(1)}, bf16[256,2048]{1,0:T(8,128)(2,1)}, u32[]{:S(2)}) copy-start(bf16[256,2048]{1,0:T(8,128)(2,1)} %matrix.1) | copy-start | bytes 3145732

commit v2 on v1

v2 whole, which is shorter than its diff:
```python
import jax
import jax.numpy as jnp
from jax import lax
from jax.experimental import pallas as pl
from jax.experimental.pallas import tpu as pltpu
from jax.sharding import PartitionSpec as P

TILE = 256
RING = 8
COLS = 8
FAN = 4
KEEP = 2
UPPER = 128
HEIGHT = 64
PIECE = 16
FAR_FIRST = (4, 3, 5, 2, 6, 1, 7)
MESH = pl.DeviceIdType.MESH


def place(step):
    step %= RING
    return 0 if step == 0 else 2 * step - 1 if step <= 4 else 2 * (RING - step)


def kernel(
    in_rows_hbm,
    keep_hbm,
    matrix,
    out,
    in_rows,
    keep,
    cols,
    lower,
    outgoing,
    pieces,
    slots,
    panel,
    infl,
    result,
    sums,
    index_sem,
    load_sem,
    p_send,
    p_recv,
    a_send,
    a_recv,
    r_send,
    r_recv,
    z_send,
    z_recv,
    s_send,
    s_recv,
    x_send,
    x_recv,
    t_send,
    t_recv,
    *bundles,
):
    rings, planes = bundles[:2], bundles[2:]
    row = lax.axis_index("wide")
    block = lax.axis_index("narrow")
    z = row // RING
    y = row % RING

    def along_y(step):
        return {"wide": z * RING + (y + step + RING) % RING}

    def along_z(step):
        return {"wide": ((z + step + RING) % RING) * RING + y}

    def along_x(step):
        return {"narrow": (block + step) % COLS}

    barrier = pltpu.get_barrier_semaphore()
    for step in range(1, RING):
        for target in (along_y(step), along_z(step), along_x(step)):
            pl.semaphore_signal(barrier, inc=1, device_id=target, device_id_type=MESH)
    indices = [
        pltpu.make_async_copy(in_rows_hbm, in_rows, index_sem.at[0]),
        pltpu.make_async_copy(keep_hbm, keep, index_sem.at[1]),
    ]
    for load in indices:
        load.start()
    loads = []
    for col in range(COLS):
        load = pltpu.make_async_copy(
            matrix.at[:, pl.ds(col * TILE, TILE)], cols.at[col], load_sem.at[col]
        )
        load.start()
        loads.append(load)
    for load in indices:
        load.wait()

    mine = jnp.int32(0)
    for col in range(COLS):
        for s in range(FAN):
            mine = jnp.where(in_rows[s, block * COLS + col] == row, col, mine)
    for load in loads:
        load.wait()
    own = cols[mine]
    panel[0] = own
    for chunk in range(2):
        rings[chunk][0] = own[chunk * HEIGHT : (chunk + 1) * HEIGHT]
    lower[...] = own[UPPER:].reshape(RING, PIECE, TILE)
    planes[0][0] = lower[y]
    pl.semaphore_wait(barrier, 3 * (RING - 1))

    started = []

    def send(src, dst, send_sem, recv_sem, target):
        copy = pltpu.make_async_remote_copy(
            src_ref=src,
            dst_ref=dst,
            send_sem=send_sem,
            recv_sem=recv_sem,
            device_id=target,
            device_id_type=MESH,
        )
        copy.start()
        started.append(copy)
        return copy

    def arrive(copies):
        for copy in copies:
            copy.wait_recv()

    parted = [
        send(
            lower.at[(y + d) % RING],
            planes[0].at[-d % RING],
            p_send.at[d - 1],
            p_recv.at[d - 1],
            along_y(d),
        )
        for d in FAR_FIRST
    ]
    spread = [
        [
            send(
                ring.at[0],
                ring.at[-d % RING],
                a_send.at[chunk, d - 1],
                a_recv.at[chunk, d - 1],
                along_y(d),
            )
            for d in FAR_FIRST
        ]
        for chunk, ring in enumerate(rings)
    ]

    def pass_on(step, refs, send_sem, recv_sem, move, size):
        first, second = (0, size), (0, size)
        if step == 4:
            first, second = (0, size // 2), (size // 2, size // 2)
        return (
            send(
                refs[(1 - step) % RING].at[pl.ds(*first)],
                refs[-step % RING].at[pl.ds(*first)],
                send_sem.at[0, step - 1],
                recv_sem.at[0, step - 1],
                move(1),
            ),
            send(
                refs[step - 1].at[pl.ds(*second)],
                refs[step].at[pl.ds(*second)],
                send_sem.at[1, step - 1],
                recv_sem.at[1, step - 1],
                move(-1),
            ),
        )

    def z_step(step):
        return pass_on(step, planes, r_send, r_recv, along_z, RING)

    gathers = [
        send(
            panel.at[0],
            panel.at[-d % COLS],
            x_send.at[d - 1],
            x_recv.at[d - 1],
            along_x(d),
        )
        for d in FAR_FIRST
    ]

    def holders(group, rows):
        found = [jnp.int32(0) for _ in rows]
        for k in range(RING):
            for t in range(FAN):
                named = in_rows[t, group * RING + k]
                for i, wanted in enumerate(rows):
                    found[i] = jnp.where(named == wanted, k, found[i])
        return [(k - y + RING) % RING for k in found]

    to_planes = holders(z, [((z + d) % RING) * RING + y for d in range(RING)])
    in_plane = [z * RING + (y + d) % RING for d in range(RING)]
    to_devices = {}
    for g in range(RING):
        to_devices[g] = holders((z + g) % RING, in_plane)

    across = []

    def hand_out(chunk):
        rows = pl.ds(chunk * HEIGHT, HEIGHT)
        for d in FAR_FIRST:
            outgoing[d, rows] = rings[chunk][to_planes[d]]
            across.append(
                send(
                    outgoing.at[d, rows],
                    slots.at[place(-d), rows],
                    z_send.at[chunk, d - 1],
                    z_recv.at[chunk, d - 1],
                    along_z(d),
                )
            )
        slots[0, rows] = rings[chunk][to_planes[0]]

    here = pl.ds(pl.multiple_of(UPPER + y * PIECE, PIECE), PIECE)

    def deal(distance):
        both = sorted({distance, -distance % RING})
        first = place(distance)
        group = pl.ds(first, len(both))
        for d in FAR_FIRST + (0,):
            for g in both:
                piece = planes[g][to_devices[g][d]]
                if d == 0:
                    slots[place(g), here] = piece
                else:
                    pieces[place(g), d] = piece
            if d:
                across.append(
                    send(
                        pieces.at[group, d],
                        slots.at[group, here],
                        s_send.at[distance, d - 1],
                        s_recv.at[distance, d - 1],
                        along_y(d),
                    )
                )

    arrive(parted)
    z_moves = z_step(1)
    deal(0)
    arrive(z_moves)
    z_moves = z_step(2)
    deal(1)
    arrive(spread[0])
    hand_out(0)
    arrive(z_moves)
    z_moves = z_step(3)
    deal(2)
    arrive(z_moves)
    z_moves = z_step(4)
    deal(3)
    arrive(spread[1])
    hand_out(1)
    arrive(z_moves)
    deal(4)

    slots[RING] = jnp.zeros((TILE, TILE), jnp.bfloat16)
    lefts, rights, kept = [], [], []
    for col in range(COLS):
        column = block * COLS + col
        is_kept = jnp.bool_(False)
        for s in range(FAN):
            inner = in_rows[s, column]
            meets = jnp.bool_(False)
            for t in range(FAN):
                names = in_rows[t, inner] == row
                meets = meets | names
                if t < KEEP:
                    if s == 0 and t == 0:
                        is_kept = is_kept | names
                    else:
                        is_kept = is_kept | (names & (keep[s, t, column] == 1))
            group = inner // RING
            lefts.append((group - block + COLS) % COLS)
            step = (group - z + RING) % RING
            slot = jnp.where(step <= 4, jnp.maximum(2 * step - 1, 0), 2 * (RING - step))
            rights.append(jnp.where(meets, slot, RING))
        kept.append(is_kept)

    arrive(gathers)
    arrive(across)

    for col in range(COLS):
        total = jnp.zeros((TILE, TILE), jnp.float32)
        for s in range(FAN):
            i = col * FAN + s
            total += jnp.dot(
                panel[lefts[i]], slots[rights[i]], preferred_element_type=jnp.float32
            )
        total = jnp.where(kept[col], total, jnp.float32(0.0))
        square = total * total
        infl[col] = square
        sums[0, pl.ds(col, 1)] = jnp.sum(square, axis=0, keepdims=True)

    def add_up(first, move):
        copies = [
            send(
                sums.at[first],
                sums.at[first + d],
                t_send.at[first + d - 1],
                t_recv.at[first + d - 1],
                move(d),
            )
            for d in FAR_FIRST
        ]
        arrive(copies)
        total = sums[first]
        for d in range(1, RING):
            total += sums[first + d]
        return total

    sums[RING] = add_up(0, along_y)
    scale = jnp.float32(TILE) / add_up(RING, along_z)
    stores = []
    for col in range(COLS):
        result[col] = (infl[col] * scale[col : col + 1]).astype(jnp.bfloat16)
        store = pltpu.make_async_copy(
            result.at[col], out.at[:, pl.ds(col * TILE, TILE)], load_sem.at[col]
        )
        store.start()
        stores.append(store)
    for copy in started:
        copy.wait_send()
    for store in stores:
        store.wait()


def on_device(matrix, in_rows, keep):
    tile = (TILE, TILE)
    bundle = (RING, PIECE, TILE)
    dma = pltpu.SemaphoreType.DMA
    others = RING - 1
    hbm = pl.BlockSpec(memory_space=pltpu.HBM)
    return pl.pallas_call(
        kernel,
        out_shape=jax.ShapeDtypeStruct(matrix.shape, jnp.bfloat16),
        in_specs=[hbm, hbm, hbm],
        out_specs=hbm,
        scratch_shapes=[
            pltpu.SMEM((FAN, in_rows.shape[0]), jnp.int32),
            pltpu.SMEM((FAN, KEEP, in_rows.shape[0]), jnp.int32),
            pltpu.VMEM((COLS, *tile), jnp.bfloat16),
            pltpu.VMEM(bundle, jnp.bfloat16),
            pltpu.VMEM((RING, UPPER, TILE), jnp.bfloat16),
            pltpu.VMEM((RING, *bundle), jnp.bfloat16),
            pltpu.VMEM((RING + 1, *tile), jnp.bfloat16),
            pltpu.VMEM((COLS, *tile), jnp.bfloat16),
            pltpu.VMEM((COLS, *tile), jnp.float32),
            pltpu.VMEM((COLS, *tile), jnp.bfloat16),
            pltpu.VMEM((2 * RING, COLS, TILE), jnp.float32),
            dma((2,)),
            dma((COLS,)),
            dma((others,)),
            dma((others,)),
            dma((2, others)),
            dma((2, others)),
            dma((2, 4)),
            dma((2, 4)),
            dma((2, others)),
            dma((2, others)),
            dma((5, others)),
            dma((5, others)),
            dma((others,)),
            dma((others,)),
            dma((2 * RING - 1,)),
            dma((2 * RING - 1,)),
            pltpu.VMEM((RING, HEIGHT, TILE), jnp.bfloat16),
            pltpu.VMEM((RING, HEIGHT, TILE), jnp.bfloat16),
            *[pltpu.VMEM(bundle, jnp.bfloat16)] * RING,
        ],
        compiler_params=pltpu.CompilerParams(
            collective_id=0, has_side_effects=True, vmem_limit_bytes=56 << 20
        ),
    )(in_rows.T, keep.transpose(1, 2, 0), matrix)


def solution(mesh):
    return jax.shard_map(
        on_device,
        mesh=mesh,
        in_specs=(P("wide", "narrow"), P(), P()),
        out_specs=P("wide", "narrow"),
        check_vma=False,
    )
```

time: 70 us -> 59.3 us (0.85); the launches traced: 69.8 us -> 58.4 us
  Pallas kernels: 66.7 us -> 56.1 us
  local copies, waits for them, and re-layouts: 3.11 us -> 2.3 us
    pallas_call x1, Pallas kernels: 66.7 us -> 56.1 us  [on_device(): pl.pallas_call(kernel, out_shape=jax.ShapeDtypeStruct(matrix.shape, jnp.b...]
    unnamed x7 -> x1, local copies, waits for them, and re-layouts: 3.11 us -> 2.3 us
where the time goes in v2:
time: 59.3 us; the launch traced here: 58.4 us
  Pallas kernels  56.1 us (95%)
  local copies, waits for them, and re-layouts  2.3 us (4%)
    pallas_call x1, Pallas kernels, on_device(): pl.pallas_call(kernel, out_shape=jax.ShapeDtypeStruct(matrix.shape, jnp.b...  56.1 us
    unnamed x1, local copies, waits for them, and re-layouts  2.3 us

profile of v2, /device:TPU:6, one launch (start us, length us, event | category | flops | bytes accessed | tf_op | source)
XLA Modules:
  0.0 58.4 jit_solution(14750875758689760159)
XLA Ops:
  0.0 56.1 %shard_map.37 = bf16[256,2048]{1,0:T(8,128)(2,1)} custom-call(s32[4,64]{1,0:T(4,128)} %bitcast.3, s32[4,2,64]{2,1,0:T(2,128)} %bitcast.2, bf16[256,2048]{1,0:T(8,128)(2,1)} %matrix.1), custom_call_target="tpu_custom_call" | custom-call | tf_op jit(solution)/shard_map/pallas_call | solution.py:338
  56.1 2.3 %copy.5 = bf16[256,2048]{1,0:T(8,128)(2,1)} copy(bf16[256,2048]{1,0:T(8,128)(2,1)} %shard_map.37) | data formatting | bytes 2097152

commit v3 on v2

--- a/solution.py
+++ b/solution.py
@@ -148,29 +148,32 @@
         for chunk, ring in enumerate(rings)
     ]
 
-    def pass_on(step, refs, send_sem, recv_sem, move, size):
-        first, second = (0, size), (0, size)
-        if step == 4:
-            first, second = (0, size // 2), (size // 2, size // 2)
-        return (
-            send(
-                refs[(1 - step) % RING].at[pl.ds(*first)],
-                refs[-step % RING].at[pl.ds(*first)],
-                send_sem.at[0, step - 1],
-                recv_sem.at[0, step - 1],
-                move(1),
-            ),
-            send(
-                refs[step - 1].at[pl.ds(*second)],
-                refs[step].at[pl.ds(*second)],
-                send_sem.at[1, step - 1],
-                recv_sem.at[1, step - 1],
-                move(-1),
-            ),
-        )
-
-    def z_step(step):
-        return pass_on(step, planes, r_send, r_recv, along_z, RING)
+    def z_send_to(source, target, move, i, part=(0, RING)):
+        return send(
+            planes[source % RING].at[pl.ds(*part)],
+            planes[target % RING].at[pl.ds(*part)],
+            r_send.at[i],
+            r_recv.at[i],
+            along_z(move),
+        )
+
+    def z_near():
+        return [
+            z_send_to(0, -2, 2, 0),
+            z_send_to(0, 2, -2, 1),
+            z_send_to(0, -1, 1, 2),
+            z_send_to(0, 1, -1, 3),
+        ]
+
+    def z_far_3():
+        return [z_send_to(-1, -3, 2, 4), z_send_to(1, 3, -2, 5)]
+
+    def z_far_4():
+        half = RING // 2
+        return [
+            z_send_to(-2, 4, 2, 6, (0, half)),
+            z_send_to(2, 4, -2, 7, (half, half)),
+        ]
 
     gathers = [
         send(
@@ -240,23 +243,22 @@
                 )
 
     arrive(parted)
-    z_moves = z_step(1)
+    near = z_near()
     deal(0)
-    arrive(z_moves)
-    z_moves = z_step(2)
+    arrive(near[2:])
+    third = z_far_3()
+    arrive(near[:2])
+    fourth = z_far_4()
     deal(1)
+    deal(2)
     arrive(spread[0])
     hand_out(0)
-    arrive(z_moves)
-    z_moves = z_step(3)
-    deal(2)
-    arrive(z_moves)
-    z_moves = z_step(4)
+    arrive(third)
     deal(3)
+    arrive(fourth)
+    deal(4)
     arrive(spread[1])
     hand_out(1)
-    arrive(z_moves)
-    deal(4)
 
     slots[RING] = jnp.zeros((TILE, TILE), jnp.bfloat16)
     lefts, rights, kept = [], [], []
@@ -296,7 +298,7 @@
         infl[col] = square
         sums[0, pl.ds(col, 1)] = jnp.sum(square, axis=0, keepdims=True)
 
-    def add_up(first, move):
+    def add_up(first, move, earlier):
         copies = [
             send(
                 sums.at[first],
@@ -307,14 +309,17 @@
             )
             for d in FAR_FIRST
         ]
+        for copy in earlier:
+            copy.wait_send()
         arrive(copies)
         total = sums[first]
         for d in range(1, RING):
             total += sums[first + d]
         return total
 
-    sums[RING] = add_up(0, along_y)
-    scale = jnp.float32(TILE) / add_up(RING, along_z)
+    sums[RING] = add_up(0, along_y, started[:])
+    last = started[-(RING - 1) :]
+    scale = jnp.float32(TILE) / add_up(RING, along_z, last)
     stores = []
     for col in range(COLS):
         result[col] = (infl[col] * scale[col : col + 1]).astype(jnp.bfloat16)
@@ -323,7 +328,7 @@
         )
         store.start()
         stores.append(store)
-    for copy in started:
+    for copy in started[-(RING - 1) :]:
         copy.wait_send()
     for store in stores:
         store.wait()
@@ -358,8 +363,8 @@
             dma((others,)),
             dma((2, others)),
             dma((2, others)),
-            dma((2, 4)),
-            dma((2, 4)),
+            dma((8,)),
+            dma((8,)),
             dma((2, others)),
             dma((2, others)),
             dma((5, others)),
@@ -373,7 +378,7 @@
             *[pltpu.VMEM(bundle, jnp.bfloat16)] * RING,
         ],
         compiler_params=pltpu.CompilerParams(
-            collective_id=0, has_side_effects=True, vmem_limit_bytes=56 << 20
+            collective_id=0, has_side_effects=True, vmem_limit_bytes=52 << 20
         ),
     )(in_rows.T, keep.transpose(1, 2, 0), matrix)
 

time: 59.3 us -> 56.2 us (0.948)
  Pallas kernels: 56.1 us -> 53.5 us
    pallas_call x1, Pallas kernels: 56.1 us -> 53.5 us  [on_device(): pl.pallas_call(kernel, out_shape=jax.ShapeDtypeStruct(matrix.shape, jnp.b...]
    unnamed x1 -> x5, local copies, waits for them, and re-layouts: 2.3 us -> 2.34 us
where the time goes in v3:
time: 56.2 us; the launch traced here: 55.8 us
  Pallas kernels  53.5 us (95%)
  local copies, waits for them, and re-layouts  2.34 us (4%)
    pallas_call x1, Pallas kernels, on_device(): pl.pallas_call(kernel, out_shape=jax.ShapeDtypeStruct(matrix.shape, jnp.b...  53.5 us
    unnamed x5, local copies, waits for them, and re-layouts  2.34 us

profile of v3, /device:TPU:6, one launch (start us, length us, event | category | flops | bytes accessed | tf_op | source)
XLA Modules:
  0.0 55.8 jit_solution(13475483304325608465)
XLA Ops:
  0.0 0.0 copy-start.1
  0.0 0.7 %copy-done.1 = s32[64,4]{0,1:T(4,128)S(1)} copy-done((s32[64,4]{0,1:T(4,128)S(1)}, s32[64,4]{0,1:T(4,128)}, u32[]{:S(2)}) %copy-start.1) | copy-done | bytes 1048
  0.7 0.0 copy-start
  0.7 0.7 %copy-done = s32[64,4,2]{0,2,1:T(2,128)S(1)} copy-done((s32[64,4,2]{0,2,1:T(2,128)S(1)}, s32[64,4,2]{0,2,1:T(2,128)}, u32[]{:S(2)}) %copy-start) | copy-done | bytes 2072
  1.4 53.5 %shard_map.37 = bf16[256,2048]{1,0:T(8,128)(2,1)S(1)} custom-call(s32[4,64]{1,0:T(4,128)S(1)} %bitcast.3, s32[4,2,64]{2,1,0:T(2,128)S(1)} %bitcast.2, bf16[256,2048]{1,0:T(8,128)(2,1)} %matrix.1), custom_call_target="tpu_custom_call" | custom-call | tf_op jit(solution)/shard_map/pallas_call | solution.py:343
  54.8 1.0 %copy.5 = bf16[256,2048]{1,0:T(8,128)(2,1)} copy(bf16[256,2048]{1,0:T(8,128)(2,1)S(1)} %shard_map.37) | data formatting | bytes 2097152
Async XLA Ops:
  0.0 0.7 %copy-start.1 = (s32[64,4]{0,1:T(4,128)S(1)}, s32[64,4]{0,1:T(4,128)}, u32[]{:S(2)}) copy-start(s32[64,4]{0,1:T(4,128)} %param.4) | copy-start | bytes 3076
  0.7 0.7 %copy-start = (s32[64,4,2]{0,2,1:T(2,128)S(1)}, s32[64,4,2]{0,2,1:T(2,128)}, u32[]{:S(2)}) copy-start(s32[64,4,2]{0,2,1:T(2,128)} %param.5) | copy-start | bytes 6148

commit v4 on v3

--- a/solution.py
+++ b/solution.py
@@ -11,7 +11,7 @@
 FAN = 4
 KEEP = 2
 UPPER = 128
-HEIGHT = 64
+CHUNKS = (64, 64)
 PIECE = 16
 FAR_FIRST = (4, 3, 5, 2, 6, 1, 7)
 MESH = pl.DeviceIdType.MESH
@@ -23,12 +23,10 @@
 
 
 def kernel(
-    in_rows_hbm,
-    keep_hbm,
+    index_hbm,
     matrix,
     out,
     in_rows,
-    keep,
     cols,
     lower,
     outgoing,
@@ -42,8 +40,8 @@
     load_sem,
     p_send,
     p_recv,
-    a_send,
-    a_recv,
+    y_send,
+    y_recv,
     r_send,
     r_recv,
     z_send,
@@ -56,7 +54,8 @@
     t_recv,
     *bundles,
 ):
-    rings, planes = bundles[:2], bundles[2:]
+    rings, planes = bundles[: len(CHUNKS)], bundles[len(CHUNKS) :]
+    starts = [sum(CHUNKS[:c]) for c in range(len(CHUNKS))]
     row = lax.axis_index("wide")
     block = lax.axis_index("narrow")
     z = row // RING
@@ -75,12 +74,8 @@
     for step in range(1, RING):
         for target in (along_y(step), along_z(step), along_x(step)):
             pl.semaphore_signal(barrier, inc=1, device_id=target, device_id_type=MESH)
-    indices = [
-        pltpu.make_async_copy(in_rows_hbm, in_rows, index_sem.at[0]),
-        pltpu.make_async_copy(keep_hbm, keep, index_sem.at[1]),
-    ]
-    for load in indices:
-        load.start()
+    index_load = pltpu.make_async_copy(index_hbm, in_rows, index_sem.at[0])
+    index_load.start()
     loads = []
     for col in range(COLS):
         load = pltpu.make_async_copy(
@@ -88,8 +83,7 @@
         )
         load.start()
         loads.append(load)
-    for load in indices:
-        load.wait()
+    index_load.wait()
 
     mine = jnp.int32(0)
     for col in range(COLS):
@@ -99,8 +93,8 @@
         load.wait()
     own = cols[mine]
     panel[0] = own
-    for chunk in range(2):
-        rings[chunk][0] = own[chunk * HEIGHT : (chunk + 1) * HEIGHT]
+    for ring, start, height in zip(rings, starts, CHUNKS):
+        ring[0] = own[start : start + height]
     lower[...] = own[UPPER:].reshape(RING, PIECE, TILE)
     planes[0][0] = lower[y]
     pl.semaphore_wait(barrier, 3 * (RING - 1))
@@ -134,47 +128,33 @@
         )
         for d in FAR_FIRST
     ]
-    spread = [
-        [
-            send(
-                ring.at[0],
-                ring.at[-d % RING],
-                a_send.at[chunk, d - 1],
-                a_recv.at[chunk, d - 1],
-                along_y(d),
+    def near(refs, send_sem, recv_sem, move):
+        return [
+            send(refs[0], refs[-d], send_sem.at[i], recv_sem.at[i], move(d))
+            for i, d in enumerate((2, -2, 1, -1))
+        ]
+
+    def far(refs, distance, size, send_sem, recv_sem, move):
+        copies = []
+        for i, way in enumerate((1, -1)):
+            part = pl.ds(0, size)
+            if distance == 4:
+                part = pl.ds(i * (size // 2), size // 2)
+            copies.append(
+                send(
+                    refs[-way * (distance - 2)].at[part],
+                    refs[-way * distance].at[part],
+                    send_sem.at[2 * distance - 2 + i],
+                    recv_sem.at[2 * distance - 2 + i],
+                    move(2 * way),
+                )
             )
-            for d in FAR_FIRST
-        ]
-        for chunk, ring in enumerate(rings)
-    ]
-
-    def z_send_to(source, target, move, i, part=(0, RING)):
-        return send(
-            planes[source % RING].at[pl.ds(*part)],
-            planes[target % RING].at[pl.ds(*part)],
-            r_send.at[i],
-            r_recv.at[i],
-            along_z(move),
-        )
-
-    def z_near():
-        return [
-            z_send_to(0, -2, 2, 0),
-            z_send_to(0, 2, -2, 1),
-            z_send_to(0, -1, 1, 2),
-            z_send_to(0, 1, -1, 3),
-        ]
-
-    def z_far_3():
-        return [z_send_to(-1, -3, 2, 4), z_send_to(1, 3, -2, 5)]
-
-    def z_far_4():
-        half = RING // 2
-        return [
-            z_send_to(-2, 4, 2, 6, (0, half)),
-            z_send_to(2, 4, -2, 7, (half, half)),
-        ]
-
+        return copies
+
+    z_sems = r_send, r_recv
+    y_sems = [(y_send.at[c], y_recv.at[c]) for c in range(len(CHUNKS))]
+    y_refs = [[ring.at[d] for d in range(RING)] for ring in rings]
+    y_near = [near(y_refs[c], *y_sems[c], along_y) for c in range(len(CHUNKS))]
     gathers = [
         send(
             panel.at[0],
@@ -204,7 +184,7 @@
     across = []
 
     def hand_out(chunk):
-        rows = pl.ds(chunk * HEIGHT, HEIGHT)
+        rows = pl.ds(starts[chunk], CHUNKS[chunk])
         for d in FAR_FIRST:
             outgoing[d, rows] = rings[chunk][to_planes[d]]
             across.append(
@@ -242,23 +222,35 @@
                     )
                 )
 
+    y_far = {}
+
+    def y_on(chunk):
+        arrive(y_near[chunk])
+        y_far[chunk] = [
+            copy
+            for distance in (3, 4)
+            for copy in far(y_refs[chunk], distance, CHUNKS[chunk], *y_sems[chunk], along_y)
+        ]
+
     arrive(parted)
-    near = z_near()
+    z_near = near(planes, *z_sems, along_z)
+    y_on(0)
+    arrive(z_near[2:])
+    z_third = far(planes, 3, RING, *z_sems, along_z)
+    y_on(1)
+    arrive(z_near[:2])
+    z_fourth = far(planes, 4, RING, *z_sems, along_z)
     deal(0)
-    arrive(near[2:])
-    third = z_far_3()
-    arrive(near[:2])
-    fourth = z_far_4()
     deal(1)
+    arrive(y_far[0])
+    hand_out(0)
     deal(2)
-    arrive(spread[0])
-    hand_out(0)
-    arrive(third)
+    arrive(z_third)
     deal(3)
-    arrive(fourth)
+    arrive(y_far[1])
+    hand_out(1)
+    arrive(z_fourth)
     deal(4)
-    arrive(spread[1])
-    hand_out(1)
 
     slots[RING] = jnp.zeros((TILE, TILE), jnp.bfloat16)
     lefts, rights, kept = [], [], []
@@ -275,7 +267,7 @@
                     if s == 0 and t == 0:
                         is_kept = is_kept | names
                     else:
-                        is_kept = is_kept | (names & (keep[s, t, column] == 1))
+                        is_kept = is_kept | (names & (in_rows[FAN + s * KEEP + t, column] == 1))
             group = inner // RING
             lefts.append((group - block + COLS) % COLS)
             step = (group - z + RING) % RING
@@ -335,6 +327,7 @@
 
 
 def on_device(matrix, in_rows, keep):
+    index = jnp.concatenate([in_rows, keep.reshape(-1, FAN * KEEP)], axis=1).T
     tile = (TILE, TILE)
     bundle = (RING, PIECE, TILE)
     dma = pltpu.SemaphoreType.DMA
@@ -343,11 +336,10 @@
     return pl.pallas_call(
         kernel,
         out_shape=jax.ShapeDtypeStruct(matrix.shape, jnp.bfloat16),
-        in_specs=[hbm, hbm, hbm],
+        in_specs=[hbm, hbm],
         out_specs=hbm,
         scratch_shapes=[
-            pltpu.SMEM((FAN, in_rows.shape[0]), jnp.int32),
-            pltpu.SMEM((FAN, KEEP, in_rows.shape[0]), jnp.int32),
+            pltpu.SMEM(index.shape, jnp.int32),
             pltpu.VMEM((COLS, *tile), jnp.bfloat16),
             pltpu.VMEM(bundle, jnp.bfloat16),
             pltpu.VMEM((RING, UPPER, TILE), jnp.bfloat16),
@@ -357,30 +349,29 @@
             pltpu.VMEM((COLS, *tile), jnp.float32),
             pltpu.VMEM((COLS, *tile), jnp.bfloat16),
             pltpu.VMEM((2 * RING, COLS, TILE), jnp.float32),
-            dma((2,)),
+            dma((1,)),
             dma((COLS,)),
             dma((others,)),
             dma((others,)),
-            dma((2, others)),
-            dma((2, others)),
+            dma((len(CHUNKS), 8)),
+            dma((len(CHUNKS), 8)),
             dma((8,)),
             dma((8,)),
-            dma((2, others)),
-            dma((2, others)),
+            dma((len(CHUNKS), others)),
+            dma((len(CHUNKS), others)),
             dma((5, others)),
             dma((5, others)),
             dma((others,)),
             dma((others,)),
             dma((2 * RING - 1,)),
             dma((2 * RING - 1,)),
-            pltpu.VMEM((RING, HEIGHT, TILE), jnp.bfloat16),
-            pltpu.VMEM((RING, HEIGHT, TILE), jnp.bfloat16),
+            *[pltpu.VMEM((RING, height, TILE), jnp.bfloat16) for height in CHUNKS],
             *[pltpu.VMEM(bundle, jnp.bfloat16)] * RING,
         ],
         compiler_params=pltpu.CompilerParams(
             collective_id=0, has_side_effects=True, vmem_limit_bytes=52 << 20
         ),
-    )(in_rows.T, keep.transpose(1, 2, 0), matrix)
+    )(index, matrix)
 
 
 def solution(mesh):

time: 56.2 us -> 54 us (0.961)
  Pallas kernels: 53.5 us -> 51.9 us
  local copies, waits for them, and re-layouts: 2.34 us -> 0.97 us
  other arithmetic: 0 us -> 0.7 us
    pallas_call x1, Pallas kernels: 53.5 us -> 51.9 us  [on_device(): pl.pallas_call(kernel, out_shape=jax.ShapeDtypeStruct(matrix.shape, jnp.b...]
    unnamed x5 -> x1, local copies, waits for them, and re-layouts: 2.34 us -> 0.97 us
    transpose x0 -> x1, other arithmetic: none -> 0.7 us  [on_device(): index = jnp.concatenate([in_rows, keep.reshape(-1, FAN * KEEP)], axis=1).T]
where the time goes in v4:
time: 54 us; the launch traced here: 53.6 us
  Pallas kernels  51.9 us (96%)
  local copies, waits for them, and re-layouts  0.97 us (2%)
  other arithmetic  0.7 us (1%)
    pallas_call x1, Pallas kernels, on_device(): pl.pallas_call(kernel, out_shape=jax.ShapeDtypeStruct(matrix.shape, jnp.b...  51.9 us

profile of v4, /device:TPU:6, one launch (start us, length us, event | category | flops | bytes accessed | tf_op | source)
XLA Modules:
  0.0 53.6 jit_solution(4945077387636034899)
XLA Ops:
  0.0 0.7 %add_bitcast_fusion.index_hbm = s32[12,64]{1,0:T(8,128)S(1)} fusion(s32[64,8]{0,1:T(8,128)} %bitcast.3, s32[64,4]{0,1:T(4,128)} %param.4), kind=kLoop, calls=%fused_computation | loop fusion | flops 768 | bytes 6144 | tf_op jit(solution)/shard_map/transpose | solution.py:330
  0.7 51.9 %shard_map.37 = bf16[256,2048]{1,0:T(8,128)(2,1)S(1)} custom-call(s32[12,64]{1,0:T(8,128)S(1)} %add_bitcast_fusion.index_hbm, bf16[256,2048]{1,0:T(8,128)(2,1)} %matrix.1), custom_call_target="tpu_custom_call" | custom-call | tf_op jit(solution)/shard_map/pallas_call | solution.py:336
  52.6 1.0 %copy.5 = bf16[256,2048]{1,0:T(8,128)(2,1)} copy(bf16[256,2048]{1,0:T(8,128)(2,1)S(1)} %shard_map.37) | data formatting | bytes 2097152

commit v5 on v4

--- a/solution.py
+++ b/solution.py
@@ -131,7 +131,7 @@
     def near(refs, send_sem, recv_sem, move):
         return [
             send(refs[0], refs[-d], send_sem.at[i], recv_sem.at[i], move(d))
-            for i, d in enumerate((2, -2, 1, -1))
+            for i, d in enumerate((1, -1, 2, -2))
         ]
 
     def far(refs, distance, size, send_sem, recv_sem, move):
@@ -235,10 +235,10 @@
     arrive(parted)
     z_near = near(planes, *z_sems, along_z)
     y_on(0)
-    arrive(z_near[2:])
+    arrive(z_near[:2])
     z_third = far(planes, 3, RING, *z_sems, along_z)
     y_on(1)
-    arrive(z_near[:2])
+    arrive(z_near[2:])
     z_fourth = far(planes, 4, RING, *z_sems, along_z)
     deal(0)
     deal(1)

time: 54 us -> 53.4 us (0.989)
  no operation moved by 1% of the time
where the time goes in v5:
time: 53.4 us; the launch traced here: 53.2 us
  Pallas kernels  51.6 us (97%)
  local copies, waits for them, and re-layouts  0.97 us (2%)
  other arithmetic  0.7 us (1%)
    pallas_call x1, Pallas kernels, on_device(): pl.pallas_call(kernel, out_shape=jax.ShapeDtypeStruct(matrix.shape, jnp.b...  51.6 us

profile of v5, /device:TPU:6, one launch (start us, length us, event | category | flops | bytes accessed | tf_op | source)
XLA Modules:
  0.0 53.2 jit_solution(12936526368025750825)
XLA Ops:
  0.0 0.7 %add_bitcast_fusion.index_hbm = s32[12,64]{1,0:T(8,128)S(1)} fusion(s32[64,8]{0,1:T(8,128)} %bitcast.3, s32[64,4]{0,1:T(4,128)} %param.4), kind=kLoop, calls=%fused_computation | loop fusion | flops 768 | bytes 6144 | tf_op jit(solution)/shard_map/transpose | solution.py:330
  0.7 51.6 %shard_map.37 = bf16[256,2048]{1,0:T(8,128)(2,1)S(1)} custom-call(s32[12,64]{1,0:T(8,128)S(1)} %add_bitcast_fusion.index_hbm, bf16[256,2048]{1,0:T(8,128)(2,1)} %matrix.1), custom_call_target="tpu_custom_call" | custom-call | tf_op jit(solution)/shard_map/pallas_call | solution.py:336
  52.3 1.0 %copy.5 = bf16[256,2048]{1,0:T(8,128)(2,1)} copy(bf16[256,2048]{1,0:T(8,128)(2,1)S(1)} %shard_map.37) | data formatting | bytes 2097152
